TPU v7x, 32 devices: a whole 2x2x4 slice. The times are simulated.
32 devices in a mesh: scen: 2 (over y), slab: 4 (over z), section: 2 (over x), pencil: 2 (over core).
Axes of the slice: x: 2, y: 2, z: 4, core: 2. Of those that a mesh axis runs over, the one named last changes fastest.
Arguments:
- checkpoint_state: float32 [5, 64, 16, 128], P(None, ('scen', 'slab', 'section'), 'pencil'), parts along dimension 1, may hold values from -6 to 6
- start_state: float32 [5, 64, 16, 128], P(None, ('scen', 'slab', 'section'), 'pencil'), parts along dimension 1, may hold values from -6 to 6
- target_temp: float32 [64, 16, 128], P(('scen', 'slab', 'section'), 'pencil'), parts along dimension 0, may hold values from -6 to 6
- zone_map: int32 [64, 16, 128], P(('scen', 'slab', 'section'), 'pencil'), parts along dimension 0, may hold values from 0 to 63, as said below
- controls_now: float32 [8, 64], P('scen'), parts along dimension 0, may hold values from -6 to 6
- controls_next: float32 [8, 64], P('scen'), parts along dimension 0, may hold values from -6 to 6
- heat_gain: float32 [64], replicated, may hold values from 0.05 to 0.3
- diffusivity: float32 [5], replicated, may hold values from 0.03 to 0.15
- coupling: float32 [5, 5], replicated, may hold values from -0.05 to 0.05
Outputs:
- end_state: float32 [5, 64, 16, 128], P(None, ('scen', 'slab', 'section'), 'pencil'), parts along dimension 1
- control_grad: float32 [8, 64], P('scen', ('slab', 'section', 'pencil')), parts along dimension 0
There are 2 independent parts, one for each index of `scen`. A program takes and returns all parts, laid end to end along the dimension named above; an argument that names none is the same for every part. Nothing has to cross between parts.
Inputs may be any that keep to these rules, and one draw needn't show every extreme that they name: `zone_map`: each zone is the cells of one box, 8 cells along the first dimension and 8 along the second, with borders along the third dimension that vary from box to box; every zone holds at least one cell and every zone number occurs.
All inputs are finite; a program needn't handle non-finite values.
Results may differ from a plain program's by a relative error of at most 0.0001.
Values sent between devices are 32-bit elements; how exact they have to be, the bound alone decides.
A program may use at most 64 MiB of HBM per device.

v0:
```python
import math

import jax
import jax.numpy as jnp
from jax import lax
from jax.sharding import PartitionSpec as P

CELLS_ZONE = 1024


def with_halo(block, sides, width):
    for axis, dim in sides:
        count = lax.axis_size(axis)
        forward = [(i, i + 1) for i in range(count - 1)]
        backward = [(target, source) for source, target in forward]
        low = lax.ppermute(
            lax.slice_in_dim(block, block.shape[dim] - width, None, axis=dim), axis, forward
        )
        high = lax.ppermute(lax.slice_in_dim(block, 0, width, axis=dim), axis, backward)
        block = jnp.concatenate([low, block, high], axis=dim)
    return block


def stencil_advance(current, diffusivity, mixing, injected, extend):
    fields = diffusivity.shape[0]
    padded = extend(current)
    beside = padded[:, 2:, 1:-1, 1:-1] + padded[:, :-2, 1:-1, 1:-1]
    beside = beside + padded[:, 1:-1, 2:, 1:-1] + padded[:, 1:-1, :-2, 1:-1]
    beside = beside + padded[:, 1:-1, 1:-1, 2:] + padded[:, 1:-1, 1:-1, :-2]
    copies = current.shape[0] // fields
    grouped = current.reshape((copies, fields) + current.shape[1:])
    beside_all = beside.reshape(grouped.shape)
    coupled = mixing[None, :, 0, None, None, None] * grouped[:, 0:1]
    for source in range(1, fields):
        coupled = (
            coupled + mixing[None, :, source, None, None, None] * grouped[:, source : source + 1]
        )
    updated = (
        grouped + diffusivity[None, :, None, None, None] * (beside_all - 6.0 * grouped) + coupled
    )
    updated = updated.at[:, 0].add(injected)
    return updated.reshape(current.shape)


def per_device(
    checkpoint_state,
    start_state,
    target_temp,
    zone_map,
    controls_now,
    controls_next,
    heat_gain,
    diffusivity,
    coupling,
):
    fields = diffusivity.shape[0]
    horizon = controls_now.shape[0]
    zone_count = heat_gain.shape[0]

    def extend(current):
        padded = with_halo(current, ((("slab", "section"), 1), ("pencil", 2)), 1)
        return jnp.pad(padded, ((0, 0), (0, 0), (0, 0), (1, 1)))

    now_table = heat_gain[None, :] * controls_now
    next_table = heat_gain[None, :] * controls_next
    misfits = []
    current = jnp.concatenate((checkpoint_state, start_state), axis=0)
    for step_index in range(horizon):
        injected = jnp.stack(
            (
                jnp.take(now_table[step_index], zone_map, axis=0),
                jnp.take(next_table[step_index], zone_map, axis=0),
            )
        )
        current = stencil_advance(current, diffusivity, coupling, injected, extend)
        misfits.append(current[0] - target_temp)
    final_state = current[fields:]
    zone_scale = heat_gain / math.sqrt(CELLS_ZONE)
    flat_zones = zone_map.reshape(-1)
    transposed = coupling.T
    adjoint = jnp.zeros_like(checkpoint_state).at[0].set(misfits[horizon - 1])
    owned = [None] * horizon
    for step_index in range(horizon - 1, -1, -1):
        if step_index < horizon - 1:
            adjoint = stencil_advance(
                adjoint, diffusivity, transposed, misfits[step_index][None], extend
            )
        terms = (
            jax.ops.segment_sum(adjoint[0].reshape(-1), flat_zones, num_segments=zone_count)
            * zone_scale
        )
        owned[step_index] = terms
    control_grad = lax.psum_scatter(
        jnp.stack(owned), ("slab", "section", "pencil"), scatter_dimension=1, tiled=True
    )
    return (final_state, control_grad)


def solution(mesh):
    return jax.shard_map(
        per_device,
        mesh=mesh,
        in_specs=(
            P(None, ("scen", "slab", "section"), "pencil", None),
            P(None, ("scen", "slab", "section"), "pencil", None),
            P(("scen", "slab", "section"), "pencil", None),
            P(("scen", "slab", "section"), "pencil", None),
            P("scen", None),
            P("scen", None),
            P(),
            P(),
            P(),
        ),
        out_specs=(
            P(None, ("scen", "slab", "section"), "pencil", None),
            P("scen", ("slab", "section", "pencil")),
        ),
        check_vma=False,
    )
```

profile of v0, /device:TPU:0, one launch (start us, length us, event | category | flops | bytes accessed | tf_op | source)
XLA Modules:
  0.0 450.1 jit_solution(16711800445082463659)
XLA Ops:
  2.9 5.6 %collective-permute-start.1 = (f32[10,1,8,128]{3,2,1,0:T(8,128)S(1)}, f32[10,1,8,128]{3,2,1,0:T(8,128)S(1)}, u32[]{:S(2)}, u32[]{:S(2)}) collective-permute-start(f32[10,1,8,128]{3,2,1,0:T(8,128)S(1)} %get-tuple-element.147), channel_id=1, source_target_pairs={{0,2},{2,4},{4,6},{6,8},{8,10},{10,12},{12,14},{1,3},{3,5},{5,7},{... | collective-permute-start | bytes 122888 | tf_op jit(solution)/shard_map/ppermute | solution.py:16
  8.6 24.7 %gather_fusion.6 = f32[4096]{0:T(1024)S(1)} fusion(f32[64]{0:T(128)S(1)} %get-tuple-element.204, s32[4096]{0:T(1024)S(1)} %bitcast_clamp_fusion), kind=kCustom, calls=%fused_computation.6.clone | custom fusion | bytes 49152 | tf_op jit(solution)/shard_map/jit(_take)/gather | solution.py:71
  33.4 24.7 %gather_fusion.2 = f32[4096]{0:T(1024)S(1)} fusion(f32[64]{0:T(128)S(1)} %get-tuple-element.203, s32[4096]{0:T(1024)S(1)} %bitcast_clamp_fusion), kind=kCustom, calls=%fused_computation.2.clone | custom fusion | bytes 49152 | tf_op jit(solution)/shard_map/jit(_take)/gather | solution.py:71
  58.1 24.7 %gather_fusion.3 = f32[4096]{0:T(1024)S(1)} fusion(f32[64]{0:T(128)S(1)} %get-tuple-element.190, s32[4096]{0:T(1024)S(1)} %bitcast_clamp_fusion), kind=kCustom, calls=%fused_computation.3.clone | custom fusion | bytes 49152 | tf_op jit(solution)/shard_map/jit(_take)/gather | solution.py:72
  82.8 24.7 %gather_fusion.4 = f32[4096]{0:T(1024)S(1)} fusion(f32[64]{0:T(128)S(1)} %get-tuple-element.205, s32[4096]{0:T(1024)S(1)} %bitcast_clamp_fusion), kind=kCustom, calls=%fused_computation.4.clone | custom fusion | bytes 49152 | tf_op jit(solution)/shard_map/jit(_take)/gather | solution.py:71
  107.5 24.7 %gather_fusion.5 = f32[4096]{0:T(1024)S(1)} fusion(f32[64]{0:T(128)S(1)} %get-tuple-element.189, s32[4096]{0:T(1024)S(1)} %bitcast_clamp_fusion), kind=kCustom, calls=%fused_computation.5.clone | custom fusion | bytes 49152 | tf_op jit(solution)/shard_map/jit(_take)/gather | solution.py:72
  132.2 24.7 %gather_fusion.7 = f32[4096]{0:T(1024)S(1)} fusion(f32[64]{0:T(128)S(1)} %get-tuple-element.188, s32[4096]{0:T(1024)S(1)} %bitcast_clamp_fusion), kind=kCustom, calls=%fused_computation.7.clone | custom fusion | bytes 49152 | tf_op jit(solution)/shard_map/jit(_take)/gather | solution.py:72
  156.9 24.7 %gather_fusion = f32[4096]{0:T(1024)S(1)} fusion(f32[64]{0:T(128)S(1)} %get-tuple-element.202, s32[4096]{0:T(1024)S(1)} %bitcast_clamp_fusion), kind=kCustom, calls=%fused_computation.clone | custom fusion | bytes 49152 | tf_op jit(solution)/shard_map/jit(_take)/gather | solution.py:71
  181.6 24.7 %gather_fusion.1 = f32[4096]{0:T(1024)S(1)} fusion(f32[64]{0:T(128)S(1)} %get-tuple-element.191, s32[4096]{0:T(1024)S(1)} %bitcast_clamp_fusion), kind=kCustom, calls=%fused_computation.1.clone | custom fusion | bytes 49152 | tf_op jit(solution)/shard_map/jit(_take)/gather | solution.py:72
  207.8 3.0 collective-permute-start.3
  214.5 5.4 %collective-permute-start.5 = (f32[10,1,8,128]{3,2,1,0:T(8,128)S(1)}, f32[10,1,8,128]{3,2,1,0:T(8,128)S(1)}, u32[]{:S(2)}, u32[]{:S(2)}) collective-permute-start(f32[10,1,8,128]{3,2,1,0:T(8,128)S(1)} %get-tuple-element.140), channel_id=1, source_target_pairs={{0,2},{2,4},{4,6},{6,8},{8,10},{10,12},{12,14},{1,3},{3,5},{5,7},{... | collective-permute-start | bytes 122888 | tf_op jit(solution)/shard_map/ppermute | solution.py:16
  222.9 3.0 collective-permute-start.7
  229.0 5.4 %collective-permute-start.9 = (f32[10,1,8,128]{3,2,1,0:T(8,128)S(1)}, f32[10,1,8,128]{3,2,1,0:T(8,128)S(1)}, u32[]{:S(2)}, u32[]{:S(2)}) collective-permute-start(f32[10,1,8,128]{3,2,1,0:T(8,128)S(1)} %get-tuple-element.134), channel_id=1, source_target_pairs={{0,2},{2,4},{4,6},{6,8},{8,10},{10,12},{12,14},{1,3},{3,5},{5,7},{... | collective-permute-start | bytes 122888 | tf_op jit(solution)/shard_map/ppermute | solution.py:16
  237.6 3.0 collective-permute-start.11
  243.7 5.7 %collective-permute-start.13 = (f32[10,1,8,128]{3,2,1,0:T(8,128)S(1)}, f32[10,1,8,128]{3,2,1,0:T(8,128)S(1)}, u32[]{:S(2)}, u32[]{:S(2)}) collective-permute-start(f32[10,1,8,128]{3,2,1,0:T(8,128)S(1)} %get-tuple-element.128), channel_id=1, source_target_pairs={{0,2},{2,4},{4,6},{6,8},{8,10},{10,12},{12,14},{1,3},{3,5},{5,7},{... | collective-permute-start | bytes 122888 | tf_op jit(solution)/shard_map/ppermute | solution.py:16
  252.4 3.0 collective-permute-start.15
  259.2 5.7 %collective-permute-start.17 = (f32[5,1,8,128]{3,2,1,0:T(8,128)S(1)}, f32[5,1,8,128]{3,2,1,0:T(8,128)S(1)}, u32[]{:S(2)}, u32[]{:S(2)}) collective-permute-start(f32[5,1,8,128]{3,2,1,0:T(8,128)S(1)} %get-tuple-element.174), channel_id=1, source_target_pairs={{0,2},{2,4},{4,6},{6,8},{8,10},{10,12},{12,14},{1,3},{3,5},{5,7},{... | collective-permute-start | bytes 61448 | tf_op jit(solution)/shard_map/ppermute | solution.py:16
  273.5 5.8 %collective-permute-start.21 = (f32[5,1,8,128]{3,2,1,0:T(8,128)S(1)}, f32[5,1,8,128]{3,2,1,0:T(8,128)S(1)}, u32[]{:S(2)}, u32[]{:S(2)}) collective-permute-start(f32[5,1,8,128]{3,2,1,0:T(8,128)S(1)} %get-tuple-element.165), channel_id=1, source_target_pairs={{0,2},{2,4},{4,6},{6,8},{8,10},{10,12},{12,14},{1,3},{3,5},{5,7},{... | collective-permute-start | bytes 61448 | tf_op jit(solution)/shard_map/ppermute | solution.py:16
  288.2 5.7 %collective-permute-start.25 = (f32[5,1,8,128]{3,2,1,0:T(8,128)S(1)}, f32[5,1,8,128]{3,2,1,0:T(8,128)S(1)}, u32[]{:S(2)}, u32[]{:S(2)}) collective-permute-start(f32[5,1,8,128]{3,2,1,0:T(8,128)S(1)} %get-tuple-element.159), channel_id=1, source_target_pairs={{0,2},{2,4},{4,6},{6,8},{8,10},{10,12},{12,14},{1,3},{3,5},{5,7},{... | collective-permute-start | bytes 61448 | tf_op jit(solution)/shard_map/ppermute | solution.py:16
  294.6 28.9 %scatter_custom_fusion.3 = f32[64]{0:T(128)S(1)} fusion(s32[4096]{0:T(1024)S(1)} %bitcast.311, f32[4096]{0:T(1024)S(1)} %get-tuple-element.123, f32[]{:T(128)} %constant.189.clone.1), kind=kCustom, calls=%fused_computation.294 | custom fusion | flops 4096 | bytes 260 | tf_op jit(solution)/shard_map/scatter-add | solution.py:89
  323.6 28.8 %scatter_custom_fusion.2 = f32[64]{0:T(128)S(1)} fusion(s32[4096]{0:T(1024)S(1)} %bitcast.312, f32[4096]{0:T(1024)S(1)} %bitcast.310, f32[]{:T(128)} %constant.189.clone.1), kind=kCustom, calls=%fused_computation.296 | custom fusion | flops 4096 | bytes 260 | tf_op jit(solution)/shard_map/scatter-add | solution.py:89
  356.8 28.8 %scatter_custom_fusion.1 = f32[64]{0:T(128)S(1)} fusion(s32[4096]{0:T(1024)S(1)} %bitcast.313, f32[4096]{0:T(1024)S(1)} %bitcast.307, f32[]{:T(128)} %constant.189.clone.1), kind=kCustom, calls=%fused_computation.298 | custom fusion | flops 4096 | bytes 260 | tf_op jit(solution)/shard_map/scatter-add | solution.py:89
  386.1 28.8 %scatter_custom_fusion = f32[64]{0:T(128)S(1)} fusion(s32[4096]{0:T(1024)S(1)} %bitcast.314, f32[4096]{0:T(1024)S(1)} %fusion.35, f32[]{:T(128)} %constant.189.clone.1), kind=kCustom, calls=%fused_computation.300 | custom fusion | flops 4096 | bytes 260 | tf_op jit(solution)/shard_map/scatter-add | solution.py:89
  414.9 34.6 %all-reduce.8 = f32[4,64]{1,0:T(4,128)S(1)} all-reduce(f32[4,64]{1,0:T(4,128)S(1)} %pad_maximum_fusion.77), channel_id=2, replica_groups=mesh['scen'=2,'slab'=4,'section'=2,'pencil'=2] {'slab','section','pencil'}, use_global_device_ids=true, to_apply=%region_4.6.clone | all-reduce | flops 256 | bytes 2048
  (129 shorter events, 49.0 us)
Async XLA Ops:
  1.6 204.8 %collective-permute-start = (f32[10,1,8,128]{3,2,1,0:T(8,128)S(1)}, f32[10,1,8,128]{3,2,1,0:T(8,128)S(1)}, u32[]{:S(2)}, u32[]{:S(2)}) collective-permute-start(f32[10,1,8,128]{3,2,1,0:T(8,128)S(1)} %get-tuple-element.148), channel_id=1, source_target_pairs={{2,0},{4,2},{6,4},{8,6},{10,8},{12,10},{14,12},{3,1},{5,3},{7,5},{... | collective-permute-start | bytes 122888 | tf_op jit(solution)/shard_map/ppermute | solution.py:19
  2.9 203.5 %collective-permute-start.1 = (f32[10,1,8,128]{3,2,1,0:T(8,128)S(1)}, f32[10,1,8,128]{3,2,1,0:T(8,128)S(1)}, u32[]{:S(2)}, u32[]{:S(2)}) collective-permute-start(f32[10,1,8,128]{3,2,1,0:T(8,128)S(1)} %get-tuple-element.147), channel_id=1, source_target_pairs={{0,2},{2,4},{4,6},{6,8},{8,10},{10,12},{12,14},{1,3},{3,5},{5,7},{... | collective-permute-start | bytes 122888 | tf_op jit(solution)/shard_map/ppermute | solution.py:16
  206.5 4.6 %collective-permute-start.2 = (f32[10,6,1,128]{3,2,1,0:T(1,128)S(1)}, f32[10,6,1,128]{3,2,1,0:T(1,128)S(1)}, u32[]{:S(2)}, u32[]{:S(2)}) collective-permute-start(f32[10,6,1,128]{3,2,1,0:T(1,128)S(1)} %get-tuple-element.115), channel_id=1, source_target_pairs={{1,0},{3,2},{5,4},{7,6},{9,8},{11,10},{13,12},{15,14},{17,16},{19,... | collective-permute-start | bytes 92168 | tf_op jit(solution)/shard_map/ppermute | solution.py:19
  207.8 3.9 collective-permute-start.3
  213.2 6.9 %collective-permute-start.4 = (f32[10,1,8,128]{3,2,1,0:T(8,128)S(1)}, f32[10,1,8,128]{3,2,1,0:T(8,128)S(1)}, u32[]{:S(2)}, u32[]{:S(2)}) collective-permute-start(f32[10,1,8,128]{3,2,1,0:T(8,128)S(1)} %get-tuple-element.141), channel_id=1, source_target_pairs={{2,0},{4,2},{6,4},{8,6},{10,8},{12,10},{14,12},{3,1},{5,3},{7,5},{... | collective-permute-start | bytes 122888 | tf_op jit(solution)/shard_map/ppermute | solution.py:19
  214.5 7.1 %collective-permute-start.5 = (f32[10,1,8,128]{3,2,1,0:T(8,128)S(1)}, f32[10,1,8,128]{3,2,1,0:T(8,128)S(1)}, u32[]{:S(2)}, u32[]{:S(2)}) collective-permute-start(f32[10,1,8,128]{3,2,1,0:T(8,128)S(1)} %get-tuple-element.140), channel_id=1, source_target_pairs={{0,2},{2,4},{4,6},{6,8},{8,10},{10,12},{12,14},{1,3},{3,5},{5,7},{... | collective-permute-start | bytes 122888 | tf_op jit(solution)/shard_map/ppermute | solution.py:16
  221.6 4.4 collective-permute-start.6
  222.9 3.9 collective-permute-start.7
  227.7 6.9 %collective-permute-start.8 = (f32[10,1,8,128]{3,2,1,0:T(8,128)S(1)}, f32[10,1,8,128]{3,2,1,0:T(8,128)S(1)}, u32[]{:S(2)}, u32[]{:S(2)}) collective-permute-start(f32[10,1,8,128]{3,2,1,0:T(8,128)S(1)} %get-tuple-element.135), channel_id=1, source_target_pairs={{2,0},{4,2},{6,4},{8,6},{10,8},{12,10},{14,12},{3,1},{5,3},{7,5},{... | collective-permute-start | bytes 122888 | tf_op jit(solution)/shard_map/ppermute | solution.py:19
  229.0 7.2 %collective-permute-start.9 = (f32[10,1,8,128]{3,2,1,0:T(8,128)S(1)}, f32[10,1,8,128]{3,2,1,0:T(8,128)S(1)}, u32[]{:S(2)}, u32[]{:S(2)}) collective-permute-start(f32[10,1,8,128]{3,2,1,0:T(8,128)S(1)} %get-tuple-element.134), channel_id=1, source_target_pairs={{0,2},{2,4},{4,6},{6,8},{8,10},{10,12},{12,14},{1,3},{3,5},{5,7},{... | collective-permute-start | bytes 122888 | tf_op jit(solution)/shard_map/ppermute | solution.py:16
  236.3 4.4 collective-permute-start.10
  242.4 7.1 %collective-permute-start.12 = (f32[10,1,8,128]{3,2,1,0:T(8,128)S(1)}, f32[10,1,8,128]{3,2,1,0:T(8,128)S(1)}, u32[]{:S(2)}, u32[]{:S(2)}) collective-permute-start(f32[10,1,8,128]{3,2,1,0:T(8,128)S(1)} %get-tuple-element.129), channel_id=1, source_target_pairs={{2,0},{4,2},{6,4},{8,6},{10,8},{12,10},{14,12},{3,1},{5,3},{7,5},{... | collective-permute-start | bytes 122888 | tf_op jit(solution)/shard_map/ppermute | solution.py:19
  243.7 7.4 %collective-permute-start.13 = (f32[10,1,8,128]{3,2,1,0:T(8,128)S(1)}, f32[10,1,8,128]{3,2,1,0:T(8,128)S(1)}, u32[]{:S(2)}, u32[]{:S(2)}) collective-permute-start(f32[10,1,8,128]{3,2,1,0:T(8,128)S(1)} %get-tuple-element.128), channel_id=1, source_target_pairs={{0,2},{2,4},{4,6},{6,8},{8,10},{10,12},{12,14},{1,3},{3,5},{5,7},{... | collective-permute-start | bytes 122888 | tf_op jit(solution)/shard_map/ppermute | solution.py:16
  251.1 4.4 collective-permute-start.14
  257.9 7.0 %collective-permute-start.16 = (f32[5,1,8,128]{3,2,1,0:T(8,128)S(1)}, f32[5,1,8,128]{3,2,1,0:T(8,128)S(1)}, u32[]{:S(2)}, u32[]{:S(2)}) collective-permute-start(f32[5,1,8,128]{3,2,1,0:T(8,128)S(1)} %get-tuple-element.175), channel_id=1, source_target_pairs={{2,0},{4,2},{6,4},{8,6},{10,8},{12,10},{14,12},{3,1},{5,3},{7,5},{... | collective-permute-start | bytes 61448 | tf_op jit(solution)/shard_map/ppermute | solution.py:19
  259.2 7.1 %collective-permute-start.17 = (f32[5,1,8,128]{3,2,1,0:T(8,128)S(1)}, f32[5,1,8,128]{3,2,1,0:T(8,128)S(1)}, u32[]{:S(2)}, u32[]{:S(2)}) collective-permute-start(f32[5,1,8,128]{3,2,1,0:T(8,128)S(1)} %get-tuple-element.174), channel_id=1, source_target_pairs={{0,2},{2,4},{4,6},{6,8},{8,10},{10,12},{12,14},{1,3},{3,5},{5,7},{... | collective-permute-start | bytes 61448 | tf_op jit(solution)/shard_map/ppermute | solution.py:16
  266.4 4.4 collective-permute-start.18
  272.2 9.0 %collective-permute-start.20 = (f32[5,1,8,128]{3,2,1,0:T(8,128)S(1)}, f32[5,1,8,128]{3,2,1,0:T(8,128)S(1)}, u32[]{:S(2)}, u32[]{:S(2)}) collective-permute-start(f32[5,1,8,128]{3,2,1,0:T(8,128)S(1)} %get-tuple-element.166), channel_id=1, source_target_pairs={{2,0},{4,2},{6,4},{8,6},{10,8},{12,10},{14,12},{3,1},{5,3},{7,5},{... | collective-permute-start | bytes 61448 | tf_op jit(solution)/shard_map/ppermute | solution.py:19
  273.5 7.7 %collective-permute-start.21 = (f32[5,1,8,128]{3,2,1,0:T(8,128)S(1)}, f32[5,1,8,128]{3,2,1,0:T(8,128)S(1)}, u32[]{:S(2)}, u32[]{:S(2)}) collective-permute-start(f32[5,1,8,128]{3,2,1,0:T(8,128)S(1)} %get-tuple-element.165), channel_id=1, source_target_pairs={{0,2},{2,4},{4,6},{6,8},{8,10},{10,12},{12,14},{1,3},{3,5},{5,7},{... | collective-permute-start | bytes 61448 | tf_op jit(solution)/shard_map/ppermute | solution.py:16
  281.2 4.4 collective-permute-start.22
  286.9 65.4 %collective-permute-start.24 = (f32[5,1,8,128]{3,2,1,0:T(8,128)S(1)}, f32[5,1,8,128]{3,2,1,0:T(8,128)S(1)}, u32[]{:S(2)}, u32[]{:S(2)}) collective-permute-start(f32[5,1,8,128]{3,2,1,0:T(8,128)S(1)} %get-tuple-element.160), channel_id=1, source_target_pairs={{2,0},{4,2},{6,4},{8,6},{10,8},{12,10},{14,12},{3,1},{5,3},{7,5},{... | collective-permute-start | bytes 61448 | tf_op jit(solution)/shard_map/ppermute | solution.py:19
  288.2 64.1 %collective-permute-start.25 = (f32[5,1,8,128]{3,2,1,0:T(8,128)S(1)}, f32[5,1,8,128]{3,2,1,0:T(8,128)S(1)}, u32[]{:S(2)}, u32[]{:S(2)}) collective-permute-start(f32[5,1,8,128]{3,2,1,0:T(8,128)S(1)} %get-tuple-element.159), channel_id=1, source_target_pairs={{0,2},{2,4},{4,6},{6,8},{8,10},{10,12},{12,14},{1,3},{3,5},{5,7},{... | collective-permute-start | bytes 61448 | tf_op jit(solution)/shard_map/ppermute | solution.py:16
  352.4 33.1 %collective-permute-start.26 = (f32[5,6,1,128]{3,2,1,0:T(1,128)S(1)}, f32[5,6,1,128]{3,2,1,0:T(1,128)S(1)}, u32[]{:S(2)}, u32[]{:S(2)}) collective-permute-start(f32[5,6,1,128]{3,2,1,0:T(1,128)S(1)} %get-tuple-element.150), channel_id=1, source_target_pairs={{1,0},{3,2},{5,4},{7,6},{9,8},{11,10},{13,12},{15,14},{17,16},{19,... | collective-permute-start | bytes 46088 | tf_op jit(solution)/shard_map/ppermute | solution.py:19
  353.7 31.8 %collective-permute-start.27 = (f32[5,6,1,128]{3,2,1,0:T(1,128)S(1)}, f32[5,6,1,128]{3,2,1,0:T(1,128)S(1)}, u32[]{:S(2)}, u32[]{:S(2)}) collective-permute-start(f32[5,6,1,128]{3,2,1,0:T(1,128)S(1)} %get-tuple-element.149), channel_id=1, source_target_pairs={{0,1},{2,3},{4,5},{6,7},{8,9},{10,11},{12,13},{14,15},{16,17},{18,... | collective-permute-start | bytes 46088 | tf_op jit(solution)/shard_map/ppermute | solution.py:16
  (13 other events, 46.8 us)
where the time goes:
time: 451 us; the launch traced here: 450 us
  local copies, waits for them, and re-layouts  203 us (45%)
  other arithmetic  121 us (27%)
  starting transfers between devices  78.6 us (17%)
  blocking collectives  34.6 us (8%)
  waiting for transfers between devices  11.3 us (3%)
    scatter-add x4, other arithmetic, per_device(): jax.ops.segment_sum(adjoint[0].reshape(-1), flat_zones, num_segments=zone...  115 us
    gather x4, local copies, waits for them, and re-layouts, per_device(): jnp.take(now_table[step_index], zone_map, axis=0)  98.8 us
    gather x4, local copies, waits for them, and re-layouts, per_device(): jnp.take(next_table[step_index], zone_map, axis=0)  98.8 us
    ppermute x14, starting transfers between devices, with_halo(): lax.ppermute(lax.slice_in_dim(block, block.shape[dim] - width, None, axis...  60.5 us
    unnamed x1, blocking collectives  34.6 us
    ppermute x14, starting transfers between devices, with_halo(): lax.ppermute(lax.slice_in_dim(block, 0, width, axis=dim), axis, backward)  18.1 us
    ppermute x14, waiting for transfers between devices, with_halo(): lax.ppermute(lax.slice_in_dim(block, block.shape[dim] - width, None, axis...  10.8 us
  transfers between devices with their start and end apart: 28, of which 13 were waited for; matrix products, arithmetic and copies ran while one was open for 63% of the time, Pallas kernels for 0%

commit v1 on v0

v1 whole, which is shorter than its diff:
```python
import functools
import math

import jax
import jax.numpy as jnp
import numpy as np
from jax import lax
from jax.experimental import pallas as pl
from jax.experimental.pallas import tpu as pltpu
from jax.sharding import PartitionSpec as P

CELLS_ZONE = 1024
BOX = 8
HIGHEST = lax.Precision.HIGHEST
MESH = pl.DeviceIdType.MESH


def laplacian_1d(n):
    return -2.0 * np.eye(n) + np.eye(n, k=1) + np.eye(n, k=-1)


def geometry(nx, ny, depth, pencils, steps):
    rows = ny // pencils
    phases = BOX // depth
    lx, ly = laplacian_1d(nx), laplacian_1d(ny)
    boxes = nx // BOX

    def powers(bx, by):
        field = np.zeros((nx, ny))
        if 0 <= bx < boxes:
            field[bx * BOX : (bx + 1) * BOX, by * BOX : (by + 1) * BOX] = 1.0
        out = []
        for _ in range(steps):
            out.append(field)
            field = lx @ field + field @ ly.T
        return out

    table = np.zeros((phases * 3 * pencils, steps * 4, steps * depth * rows), np.float32)
    for phase in range(phases):
        side = -1 if 2 * phase < phases else 1
        for edge, bx in enumerate((0, boxes // 2, boxes - 1)):
            x0 = bx * BOX + phase * depth
            for pencil in range(pencils):
                for xb in range(2):
                    for yb in range(2):
                        fields = powers(bx + side * xb, pencil if yb == 0 else 1 - pencil)
                        for r in range(steps):
                            block = fields[r][x0 : x0 + depth, pencil * rows : (pencil + 1) * rows]
                            table[(phase * 3 + edge) * pencils + pencil, r * 4 + xb * 2 + yb] = (
                                np.tile(block.reshape(-1), steps)
                            )
    return table


def kernel(
    cfg,
    check_ref,
    start_ref,
    target_ref,
    zone_ref,
    now_ref,
    next_ref,
    gain_ref,
    diff_ref,
    coup_ref,
    geo_ref,
    end_ref,
    grad_ref,
    halo,
    zhalo,
    qbuf,
    sums,
    got,
    halo_send,
    halo_recv,
    sum_send,
    sum_recv,
):
    nslab, nsec, npen, F, depth, NZ, K, zones = cfg
    nline = nslab * nsec
    count = nline * npen
    own = zones // count
    hops = -(-K // depth)
    phases = BOX // depth
    pencil = lax.axis_index("pencil")
    line = lax.axis_index("slab") * nsec + lax.axis_index("section")
    me = line * npen + pencil

    def where_is(at, pen):
        return {"slab": at // nsec, "section": at % nsec, "pencil": pen}

    slots = {}
    for off in range(-hops, hops + 1):
        for other in range(2):
            if (off, other) != (0, 0):
                slots[(off, other)] = len(slots)
    nslots = len(slots)

    barrier = pltpu.get_barrier_semaphore()

    def greet(r, carry):
        peer = lax.rem(me + r, count)
        pl.semaphore_signal(
            barrier, inc=1, device_id=where_is(peer // npen, peer % npen), device_id_type=MESH
        )
        return carry

    lax.fori_loop(1, count, greet, 0)
    pl.semaphore_wait(barrier, count - 1)

    pieces = (
        (zone_ref.at[0], lambda slot: zhalo.at[slot]),
        (check_ref, lambda slot: halo.at[0, slot]),
        (start_ref, lambda slot: halo.at[1, slot]),
    )

    def copy_to(what, off, other, arriving):
        here = slots[(off, other)]
        slot = here if arriving else slots[(-off, other)]
        src, dst = pieces[what]
        return pltpu.make_async_remote_copy(
            src_ref=src,
            dst_ref=dst(slot),
            send_sem=halo_send.at[what, here],
            recv_sem=halo_recv.at[what, slot],
            device_id=where_is(line + off, pencil if other == 0 else 1 - pencil),
            device_id_type=MESH,
        )

    def exists(off):
        return jnp.logical_and(line + off >= 0, line + off < nline)

    for what in range(3):
        for off, other in slots:

            @pl.when(exists(off))
            def _(off=off, other=other, what=what):
                copy_to(what, off, other, False).start()

    for off, other in slots:
        if off != 0:
            slot = slots[(off, other)]

            @pl.when(jnp.logical_not(exists(off)))
            def _(slot=slot):
                halo[0, slot] = jnp.zeros_like(halo[0, slot])
                halo[1, slot] = jnp.zeros_like(halo[1, slot])
                zhalo[slot] = jnp.zeros_like(zhalo[slot])

    diff = [diff_ref[f] for f in range(F)]
    coup = [[coup_ref[f, g] for g in range(F)] for f in range(F)]
    mix = [
        [coup[f][g] + (1.0 - 6.0 * diff[f]) if f == g else coup[f][g] for g in range(F)]
        for f in range(F)
    ]
    alpha = {(0, 0): jnp.float32(1.0)}
    rows = {0: [jnp.float32(1.0) if f == 0 else None for f in range(F)]}
    for p in range(1, K):
        new = {}
        for q in range(p + 1):
            vec = []
            for g in range(F):
                total = None
                if q in rows:
                    for f in range(F):
                        v = rows[q][f]
                        if v is not None:
                            c = coup[f][g] + 1.0 if f == g else coup[f][g]
                            total = v * c if total is None else total + v * c
                if q - 1 in rows and rows[q - 1][g] is not None:
                    v = rows[q - 1][g] * diff[g]
                    total = v if total is None else total + v
                vec.append(total)
            new[q] = vec
        rows = new
        for q in range(p + 1):
            alpha[(p, q)] = rows[q][0]

    lanes = K * depth * BOX
    wide = K * own
    shape = (wide, lanes)
    age = (
        lax.broadcasted_iota(jnp.int32, shape, 1) // (depth * BOX)
        - lax.broadcasted_iota(jnp.int32, shape, 0) // own
    )
    poly = []
    for q in range(K):
        part = jnp.zeros(shape, jnp.float32)
        for p in range(q, K):
            part = jnp.where(age == p, alpha[(p, q)], part)
        poly.append(part)
    phase = line % phases
    edge = jnp.where(line < phases, 0, jnp.where(line >= nline - phases, 2, 1))
    geo = geo_ref[(phase * 3 + edge) * npen + pencil]
    weights = []
    for c in range(K):
        for box in range(4):
            total = None
            for r in range(K - c):
                term = (math.comb(r + c, c) * poly[r + c]) * geo[r * 4 + box : r * 4 + box + 1]
                total = term if total is None else total + term
            weights.append(total)
    weights = jnp.concatenate(weights, axis=0)

    lane = lax.broadcasted_iota(jnp.int32, (BOX, NZ), 1)
    row = lax.broadcasted_iota(jnp.int32, (BOX, NZ), 0)
    not_first, not_last = lane > 0, lane < NZ - 1
    top, bottom = row == BOX - 1, row == 0
    half = BOX // 2
    beyond = row // half == pencil

    def along_z(v):
        low = jnp.where(not_first[: v.shape[0]], pltpu.roll(v, 1, 1), 0.0)
        high = jnp.where(not_last[: v.shape[0]], pltpu.roll(v, NZ - 1, 1), 0.0)
        return low + high

    gain = gain_ref[...].reshape(1, zones)
    tables = jnp.concatenate(
        [
            now_ref[...] * gain,
            next_ref[...] * gain,
            jnp.broadcast_to(gain * (1.0 / math.sqrt(CELLS_ZONE)), (BOX, zones)),
        ],
        axis=0,
    )

    def inject(zrow, slot):
        zone = lax.broadcasted_iota(jnp.int32, (zones, NZ), 0)
        hot = (zone == jnp.broadcast_to(zrow, (zones, NZ))).astype(jnp.float32)
        qbuf[slot] = jnp.dot(tables, hot, precision=HIGHEST, preferred_element_type=jnp.float32)

    inject(zone_ref[0][0:1], nslots)

    for off, other in slots:

        @pl.when(exists(off))
        def _(off=off, other=other):
            copy = copy_to(0, off, other, True)
            copy.wait_send()
            copy.wait_recv()

    for off, other in slots:
        slot = slots[(off, other)]
        inject(zhalo[slot][0:1], slot)

    inside = {off: jnp.where(exists(off), 1.0, 0.0) for off in range(-hops, hops + 1)}

    def off_of(plane):
        return plane // depth

    def forward(which, ref, seen):
        def plane_of(f, plane, other):
            off = off_of(plane)
            if off == 0 and other == 0:
                return ref[f, plane]
            v = halo[which, slots[(off, other)], f, plane - off * depth]
            return jnp.where(beyond, v, 0.0) if other else v

        T = [{p: plane_of(f, p, 0) for p in range(-K, depth + K)} for f in range(F)]
        U = [{p: plane_of(f, p, 1) for p in range(1 - K, depth + K - 1)} for f in range(F)]
        for step in range(K):
            reach = K - 1 - step
            newT = [{} for _ in range(F)]
            newU = [{} for _ in range(F)]
            for p in range(-reach, depth + reach):
                off = off_of(p)
                both = -reach < p < depth + reach - 1
                qt = qbuf[nslots if off == 0 else slots[(off, 0)], which * K + step : which * K + step + 1]
                if both:
                    qu = qbuf[slots[(off, 1)], which * K + step : which * K + step + 1]
                for f in range(F):
                    t, u = T[f][p], U[f][p]
                    tu, td = pltpu.roll(t, BOX - 1, 0), pltpu.roll(t, 1, 0)
                    uu, ud = pltpu.roll(u, BOX - 1, 0), pltpu.roll(u, 1, 0)
                    beside = T[f][p - 1] + T[f][p + 1] + along_z(t)
                    beside = beside + jnp.where(top, uu, tu) + jnp.where(bottom, ud, td)
                    v = diff[f] * beside
                    for g in range(F):
                        v = v + mix[f][g] * T[g][p]
                    if f == 0:
                        v = v + qt
                    if off != 0:
                        v = v * inside[off]
                    newT[f][p] = v
                    if both:
                        beside = U[f][p - 1] + U[f][p + 1] + along_z(u)
                        beside = beside + jnp.where(top, tu, uu) + jnp.where(bottom, td, ud)
                        v = diff[f] * beside
                        for g in range(F):
                            v = v + mix[f][g] * U[g][p]
                        if f == 0:
                            v = v + qu
                        if off != 0:
                            v = v * inside[off]
                        newU[f][p] = jnp.where(beyond, v, 0.0)
            T, U = newT, newU
            seen(T)
        return T

    def wait_halo(what):
        for off, other in slots:

            @pl.when(exists(off))
            def _(off=off, other=other):
                copy = copy_to(what, off, other, True)
                copy.wait_send()
                copy.wait_recv()

    wait_halo(1)
    misfits = []

    def seen(T):
        for p in range(depth):
            misfits.append(T[0][p] - target_ref[p])

    forward(0, check_ref, seen)
    R = jnp.dot(
        weights,
        jnp.concatenate(misfits, axis=0),
        precision=HIGHEST,
        preferred_element_type=jnp.float32,
    )
    zlane = lax.broadcasted_iota(jnp.int32, (wide, NZ), 1)
    side = jnp.where(2 * phase < phases, -(phase + 1), phases - phase)
    lhs, rhs = [], []
    for box in range(4):
        acc = None
        for c in range(K - 1, -1, -1):
            part = R[(c * 4 + box) * wide : (c * 4 + box + 1) * wide]
            if acc is None:
                acc = part
            else:
                low = jnp.where(zlane > 0, pltpu.roll(acc, 1, 1), 0.0)
                high = jnp.where(zlane < NZ - 1, pltpu.roll(acc, NZ - 1, 1), 0.0)
                acc = part + (low + high - 2.0 * acc)
        xb, yb = box // 2, box % 2
        if xb == 0:
            slot = nslots if yb == 0 else slots[(0, 1)]
            zrow = zone_ref[0][0:1] if yb == 0 else zhalo[slot][0:1]
        else:
            slot = jnp.int32(0)
            for off in range(-hops, hops + 1):
                if off != 0:
                    slot = jnp.where(side == off, slots[(off, yb)], slot)
            zrow = zhalo[slot][0:1]
        rhs.append(acc * qbuf[slot][2 * K : 2 * K + 1])
        owner = lax.broadcasted_iota(jnp.int32, (own * count, NZ), 0)
        number = lax.rem(owner, count) * own + owner // count
        lhs.append((number == jnp.broadcast_to(zrow, number.shape)).astype(jnp.float32))
    S = None
    for a, b in zip(lhs, rhs):
        part = lax.dot_general(
            a, b, (((1,), (1,)), ((), ())), precision=HIGHEST, preferred_element_type=jnp.float32
        )
        S = part if S is None else S + part
    pick = lax.broadcasted_iota(jnp.int32, (count, wide), 1) % own
    mine = S[:count]
    for zz in range(1, own):
        mine = jnp.where(pick == zz, S[zz * count : (zz + 1) * count], mine)
    mine = jnp.concatenate([mine, jnp.zeros((count, 128 - wide), jnp.float32)], axis=1)
    for o in range(count):
        sums[o] = mine[o : o + 1]

    def give(r, carry):
        peer = lax.rem(me + r, count)
        pltpu.make_async_remote_copy(
            src_ref=sums.at[peer],
            dst_ref=got.at[r - 1],
            send_sem=sum_send,
            recv_sem=sum_recv,
            device_id=where_is(peer // npen, peer % npen),
            device_id_type=MESH,
        ).start()
        return carry

    lax.fori_loop(1, count, give, 0)

    wait_halo(2)
    T = forward(1, start_ref, lambda T: None)
    for f in range(F):
        for p in range(depth):
            end_ref[f, p] = T[f][p]

    pltpu.make_async_copy(got, got, sum_recv).wait()
    pltpu.make_async_copy(got, got, sum_send).wait()
    total = sums[me] + jnp.sum(got[...], axis=0)
    for k in range(K):
        grad_ref[k : k + 1, :] = total[:, k * own : (k + 1) * own]


def solution(mesh):
    nslab, nsec, npen = mesh.shape["slab"], mesh.shape["section"], mesh.shape["pencil"]

    def per_device(check, start, target, zone, now, nxt, gain, diff, coup):
        F, depth, rows, NZ = check.shape
        K, zones = now.shape
        nline = nslab * nsec
        count = nline * npen
        hops = -(-K // depth)
        nslots = 2 * (2 * hops + 1) - 1
        table = jnp.asarray(geometry(nline * depth, npen * rows, depth, npen, K))
        cfg = (nslab, nsec, npen, F, depth, NZ, K, zones)
        vmem = pl.BlockSpec(memory_space=pltpu.VMEM)
        smem = pl.BlockSpec(memory_space=pltpu.SMEM)
        return pl.pallas_call(
            functools.partial(kernel, cfg),
            out_shape=(
                jax.ShapeDtypeStruct(check.shape, jnp.float32),
                jax.ShapeDtypeStruct((K, zones // count), jnp.float32),
            ),
            in_specs=[vmem] * 7 + [smem] * 2 + [vmem],
            out_specs=(vmem, vmem),
            scratch_shapes=[
                pltpu.VMEM((2, nslots, F, depth, rows, NZ), jnp.float32),
                pltpu.VMEM((nslots, rows, NZ), jnp.int32),
                pltpu.VMEM((nslots + 1, 2 * K + 8, NZ), jnp.float32),
                pltpu.VMEM((count, 1, 128), jnp.float32),
                pltpu.VMEM((count - 1, 1, 128), jnp.float32),
                pltpu.SemaphoreType.DMA((3, nslots)),
                pltpu.SemaphoreType.DMA((3, nslots)),
                pltpu.SemaphoreType.DMA,
                pltpu.SemaphoreType.DMA,
            ],
            compiler_params=pltpu.CompilerParams(
                collective_id=0, has_side_effects=True, vmem_limit_bytes=32 * 1024 * 1024
            ),
        )(check, start, target, zone, now, nxt, gain, diff, coup, table)

    return jax.shard_map(
        per_device,
        mesh=mesh,
        in_specs=(
            P(None, ("scen", "slab", "section"), "pencil", None),
            P(None, ("scen", "slab", "section"), "pencil", None),
            P(("scen", "slab", "section"), "pencil", None),
            P(("scen", "slab", "section"), "pencil", None),
            P("scen", None),
            P("scen", None),
            P(),
            P(),
            P(),
        ),
        out_specs=(
            P(None, ("scen", "slab", "section"), "pencil", None),
            P("scen", ("slab", "section", "pencil")),
        ),
        check_vma=False,
    )
```

time: 451 us -> 33.9 us (0.08)
  local copies, waits for them, and re-layouts: 203 us -> 8.67 us
  other arithmetic: 121 us -> 0 us
  starting transfers between devices: 78.6 us -> 0 us
  blocking collectives: 34.6 us -> 0 us
  Pallas kernels: 0 us -> 24.1 us
  waiting for transfers between devices: 11.3 us -> 0 us
    gather x8 -> x0, local copies, waits for them, and re-layouts: 198 us -> none  [the longest x4 98.8 us: per_device(): jnp.take(now_table[step_index], zone_map, axis=0)]
    scatter-add x6 -> x0, other arithmetic: 115 us -> none  [the longest x4 115 us: per_device(): jax.ops.segment_sum(adjoint[0].reshape(-1), flat_zones, num_segments=zone...]
    ppermute x28 -> x0, starting transfers between devices: 78.6 us -> none  [the longest x14 60.5 us: with_halo(): lax.ppermute(lax.slice_in_dim(block, block.shape[dim] - width, None, axis...]
    unnamed x1 -> x0, blocking collectives: 34.6 us -> none
    pallas_call x0 -> x1, Pallas kernels: none -> 24.1 us  [per_device(): pl.pallas_call(functools.partial(kernel, cfg), out_shape=(jax.ShapeDtypeS...]
    ppermute x28 -> x0, waiting for transfers between devices: 11.3 us -> none  [the longest x14 10.8 us: with_halo(): lax.ppermute(lax.slice_in_dim(block, block.shape[dim] - width, None, axis...]
  transfers between devices with their start and end apart: 28 -> 0, of which waited for: 13 -> 0; matrix products, arithmetic and copies ran while one was open for 63% -> 0% of each run, Pallas kernels for 0% -> 0%
where the time goes in v1:
time: 33.9 us; the launch traced here: 33.4 us
  Pallas kernels  24.1 us (71%)
  local copies, waits for them, and re-layouts  8.67 us (26%)
  between operations  0.66 us (2%)
    pallas_call x1, Pallas kernels, per_device(): pl.pallas_call(functools.partial(kernel, cfg), out_shape=(jax.ShapeDtypeS...  24.1 us
    unnamed x22, local copies, waits for them, and re-layouts  8.67 us

profile of v1, /device:TPU:0, one launch (start us, length us, event | category | flops | bytes accessed | tf_op | source)
XLA Modules:
  0.0 33.4 jit_solution(16659064310970601091)
XLA Ops:
  0.6 0.0 copy-start
  0.6 0.9 %copy-done = f32[12,16,128]{2,1,0:T(8,128)S(1)} copy-done((f32[12,16,128]{2,1,0:T(8,128)S(1)}, f32[12,16,128]{2,1,0:T(8,128)}, u32[]{:S(2)}) %copy-start) | copy-done | bytes 98328
  1.5 0.0 copy-start.1
  1.5 0.9 %copy-done.1 = f32[5,4,8,128]{3,2,1,0:T(8,128)S(1)} copy-done((f32[5,4,8,128]{3,2,1,0:T(8,128)S(1)}, f32[5,4,8,128]{3,2,1,0:T(8,128)}, u32[]{:S(2)}) %copy-start.1) | copy-done | bytes 81944
  2.4 0.0 copy-start.2
  2.4 0.9 %copy-done.2 = f32[5,4,8,128]{3,2,1,0:T(8,128)S(1)} copy-done((f32[5,4,8,128]{3,2,1,0:T(8,128)S(1)}, f32[5,4,8,128]{3,2,1,0:T(8,128)}, u32[]{:S(2)}) %copy-start.2) | copy-done | bytes 81944
  3.3 0.0 copy-start.3
  3.3 0.7 %copy-done.3 = f32[4,8,128]{2,1,0:T(8,128)S(1)} copy-done((f32[4,8,128]{2,1,0:T(8,128)S(1)}, f32[4,8,128]{2,1,0:T(8,128)}, u32[]{:S(2)}) %copy-start.3) | copy-done | bytes 16408
  4.0 0.0 copy-start.4
  4.0 0.7 %copy-done.4 = s32[4,8,128]{2,1,0:T(8,128)S(1)} copy-done((s32[4,8,128]{2,1,0:T(8,128)S(1)}, s32[4,8,128]{2,1,0:T(8,128)}, u32[]{:S(2)}) %copy-start.4) | copy-done | bytes 16408
  4.7 0.0 copy-start.5
  4.7 0.7 %copy-done.5 = f32[5,5]{1,0:T(8,128)S(1)} copy-done((f32[5,5]{1,0:T(8,128)S(1)}, f32[5,5]{1,0:T(8,128)}, u32[]{:S(2)}) %copy-start.5) | copy-done | bytes 124
  5.4 0.0 copy-start.6
  5.4 0.7 %copy-done.6 = f32[4,64]{1,0:T(4,128)S(1)} copy-done((f32[4,64]{1,0:T(4,128)S(1)}, f32[4,64]{1,0:T(4,128)}, u32[]{:S(2)}) %copy-start.6) | copy-done | bytes 1048
  6.1 0.0 copy-start.7
  6.1 0.7 %copy-done.7 = f32[4,64]{1,0:T(4,128)S(1)} copy-done((f32[4,64]{1,0:T(4,128)S(1)}, f32[4,64]{1,0:T(4,128)}, u32[]{:S(2)}) %copy-start.7) | copy-done | bytes 1048
  6.8 0.0 copy-start.8
  6.8 0.7 %copy-done.8 = f32[64]{0:T(128)S(1)} copy-done((f32[64]{0:T(128)S(1)}, f32[64]{0:T(128)}, u32[]{:S(2)}) %copy-start.8) | copy-done | bytes 280
  7.4 0.0 copy-start.9
  7.4 0.7 %copy-done.9 = f32[5]{0:T(128)S(1)} copy-done((f32[5]{0:T(128)S(1)}, f32[5]{0:T(128)}, u32[]{:S(2)}) %copy-start.9) | copy-done | bytes 44
  8.1 24.1 %shard_map.113 = (f32[5,4,8,128]{3,2,1,0:T(8,128)S(1)}, f32[4,4]{1,0:T(4,128)S(1)}) custom-call(f32[5,4,8,128]{3,2,1,0:T(8,128)S(1)} %copy-done.1, f32[5,4,8,128]{3,2,1,0:T(8,128)S(1)} %copy-done.2, f32[4,8,128]{2,1,0:T(8,128)S(1)} %copy-done.3, s32[4,8,128]{2,1,0:T(8,128)S(1)} %copy-done.4, f32[4,64]{1,0:T(4,128)S(1)} %copy-done.6, f32[4,64]{1,0:T(4,128)S(1)} %copy-done.7, ...), custom_call_target="tpu_custom_call" | custom-call | tf_op jit(solution)/shard_map/pallas_call | solution.py:405
  32.2 0.6 %copy.14 = f32[5,4,8,128]{3,2,1,0:T(8,128)} copy(f32[5,4,8,128]{3,2,1,0:T(8,128)S(1)} %get-tuple-element.4) | data formatting | bytes 163840
  32.8 0.6 %copy.15 = f32[4,4]{1,0:T(4,128)} copy(f32[4,4]{1,0:T(4,128)S(1)} %get-tuple-element.5) | data formatting | bytes 128
Async XLA Ops:
  0.6 0.9 %copy-start = (f32[12,16,128]{2,1,0:T(8,128)S(1)}, f32[12,16,128]{2,1,0:T(8,128)}, u32[]{:S(2)}) copy-start(f32[12,16,128]{2,1,0:T(8,128)} %constant.2.clone.geo_ref) | copy-start | bytes 294916
  1.5 0.9 %copy-start.1 = (f32[5,4,8,128]{3,2,1,0:T(8,128)S(1)}, f32[5,4,8,128]{3,2,1,0:T(8,128)}, u32[]{:S(2)}) copy-start(f32[5,4,8,128]{3,2,1,0:T(8,128)} %check_ref.1) | copy-start | bytes 245764
  2.4 0.9 %copy-start.2 = (f32[5,4,8,128]{3,2,1,0:T(8,128)S(1)}, f32[5,4,8,128]{3,2,1,0:T(8,128)}, u32[]{:S(2)}) copy-start(f32[5,4,8,128]{3,2,1,0:T(8,128)} %start_ref.1) | copy-start | bytes 245764
  3.3 0.7 %copy-start.3 = (f32[4,8,128]{2,1,0:T(8,128)S(1)}, f32[4,8,128]{2,1,0:T(8,128)}, u32[]{:S(2)}) copy-start(f32[4,8,128]{2,1,0:T(8,128)} %target_ref.1) | copy-start | bytes 49156
  4.0 0.7 %copy-start.4 = (s32[4,8,128]{2,1,0:T(8,128)S(1)}, s32[4,8,128]{2,1,0:T(8,128)}, u32[]{:S(2)}) copy-start(s32[4,8,128]{2,1,0:T(8,128)} %zone_ref.1) | copy-start | bytes 49156
  4.7 0.7 %copy-start.5 = (f32[5,5]{1,0:T(8,128)S(1)}, f32[5,5]{1,0:T(8,128)}, u32[]{:S(2)}) copy-start(f32[5,5]{1,0:T(8,128)} %coup_ref.1) | copy-start | bytes 304
  5.4 0.7 %copy-start.6 = (f32[4,64]{1,0:T(4,128)S(1)}, f32[4,64]{1,0:T(4,128)}, u32[]{:S(2)}) copy-start(f32[4,64]{1,0:T(4,128)} %now_ref.1) | copy-start | bytes 3076
  6.1 0.7 %copy-start.7 = (f32[4,64]{1,0:T(4,128)S(1)}, f32[4,64]{1,0:T(4,128)}, u32[]{:S(2)}) copy-start(f32[4,64]{1,0:T(4,128)} %next_ref.1) | copy-start | bytes 3076
  6.8 0.7 %copy-start.8 = (f32[64]{0:T(128)S(1)}, f32[64]{0:T(128)}, u32[]{:S(2)}) copy-start(f32[64]{0:T(128)} %gain_ref.1) | copy-start | bytes 772
  7.4 0.7 %copy-start.9 = (f32[5]{0:T(128)S(1)}, f32[5]{0:T(128)}, u32[]{:S(2)}) copy-start(f32[5]{0:T(128)} %diff_ref.1) | copy-start | bytes 64

commit v2 on v1

--- a/solution.py
+++ b/solution.py
@@ -54,6 +54,18 @@
 
 def kernel(
     cfg,
+    check_hbm,
+    start_hbm,
+    target_hbm,
+    zone_hbm,
+    now_hbm,
+    next_hbm,
+    gain_hbm,
+    diff_hbm,
+    coup_hbm,
+    geo_hbm,
+    end_ref,
+    grad_ref,
     check_ref,
     start_ref,
     target_ref,
@@ -64,13 +76,14 @@
     diff_ref,
     coup_ref,
     geo_ref,
-    end_ref,
-    grad_ref,
+    packed,
     halo,
+    corner,
     zhalo,
     qbuf,
     sums,
     got,
+    load_sem,
     halo_send,
     halo_recv,
     sum_send,
@@ -85,6 +98,28 @@
     pencil = lax.axis_index("pencil")
     line = lax.axis_index("slab") * nsec + lax.axis_index("section")
     me = line * npen + pencil
+    phase = line % phases
+    edge = jnp.where(line < phases, 0, jnp.where(line >= nline - phases, 2, 1))
+
+    loads = [
+        pltpu.make_async_copy(src, dst, load_sem.at[n])
+        for n, (src, dst) in enumerate(
+            (
+                (check_hbm, check_ref),
+                (start_hbm, start_ref),
+                (coup_hbm, coup_ref),
+                (diff_hbm, diff_ref),
+                (geo_hbm.at[(phase * 3 + edge) * npen + pencil], geo_ref),
+                (gain_hbm, gain_ref),
+                (now_hbm, now_ref),
+                (next_hbm, next_ref),
+                (zone_hbm.at[0], zone_ref),
+                (target_hbm, target_ref),
+            )
+        )
+    ]
+    for load in loads:
+        load.start()
 
     def where_is(at, pen):
         return {"slab": at // nsec, "section": at % nsec, "pencil": pen}
@@ -106,30 +141,79 @@
         return carry
 
     lax.fori_loop(1, count, greet, 0)
+
+    def exists(off):
+        return jnp.logical_and(line + off >= 0, line + off < nline)
+
+    for off, other in slots:
+        if off != 0:
+            slot = slots[(off, other)]
+
+            @pl.when(jnp.logical_not(exists(off)))
+            def _(slot=slot, other=other):
+                for which in range(2):
+                    if other:
+                        corner[which, slot] = jnp.zeros_like(corner[which, slot])
+                    else:
+                        halo[which, slot] = jnp.zeros_like(halo[which, slot])
+                zhalo[slot] = jnp.zeros_like(zhalo[slot])
+
+    row = lax.broadcasted_iota(jnp.int32, (BOX, NZ), 0)
+
+    def near(pen, at):
+        return jnp.where(pen == 0, BOX - 1 - at, at)
+
+    def turned(v, pen, back):
+        first, second = (3, 5) if back else (5, 3)
+        return jnp.where(pen == 0, pltpu.roll(v, first, 0), pltpu.roll(v, second, 0))
+
+    near_1 = near(pencil, row) < 3
+    near_2 = near(pencil, (row + 4) % BOX) < 2
+
+    def plane_at(off, distance):
+        plane = abs(off) * depth - distance
+        plane = plane if off > 0 else depth - 1 - plane
+        return plane if 0 <= plane < depth else None
+
+    def pack(which, ref):
+        for off in range(-hops, hops + 1):
+            if off == 0:
+                continue
+            one, two, three = (plane_at(off, d) for d in (1, 2, 3))
+            for f in range(F):
+                tile = jnp.zeros((BOX, NZ), jnp.float32)
+                if three is not None:
+                    tile = turned(ref[f, three], pencil, False)
+                if two is not None:
+                    tile = jnp.where(near_2, pltpu.roll(ref[f, two], 4, 0), tile)
+                if one is not None:
+                    tile = jnp.where(near_1, ref[f, one], tile)
+                packed[which, slots[(off, 1)], f] = tile
+
+    loads[0].wait()
+    pack(0, check_ref)
+    loads[1].wait()
+    pack(1, start_ref)
     pl.semaphore_wait(barrier, count - 1)
-
-    pieces = (
-        (zone_ref.at[0], lambda slot: zhalo.at[slot]),
-        (check_ref, lambda slot: halo.at[0, slot]),
-        (start_ref, lambda slot: halo.at[1, slot]),
-    )
 
     def copy_to(what, off, other, arriving):
         here = slots[(off, other)]
         slot = here if arriving else slots[(-off, other)]
-        src, dst = pieces[what]
+        if what == 0:
+            src, dst = zone_hbm.at[0], zhalo.at[slot]
+        elif off != 0 and other:
+            src, dst = packed.at[what - 1, here], corner.at[what - 1, slot]
+        else:
+            src, dst = (check_hbm, start_hbm)[what - 1], halo.at[what - 1, slot]
         return pltpu.make_async_remote_copy(
             src_ref=src,
-            dst_ref=dst(slot),
+            dst_ref=dst,
             send_sem=halo_send.at[what, here],
             recv_sem=halo_recv.at[what, slot],
             device_id=where_is(line + off, pencil if other == 0 else 1 - pencil),
             device_id_type=MESH,
         )
 
-    def exists(off):
-        return jnp.logical_and(line + off >= 0, line + off < nline)
-
     for what in range(3):
         for off, other in slots:
 
@@ -137,15 +221,8 @@
             def _(off=off, other=other, what=what):
                 copy_to(what, off, other, False).start()
 
-    for off, other in slots:
-        if off != 0:
-            slot = slots[(off, other)]
-
-            @pl.when(jnp.logical_not(exists(off)))
-            def _(slot=slot):
-                halo[0, slot] = jnp.zeros_like(halo[0, slot])
-                halo[1, slot] = jnp.zeros_like(halo[1, slot])
-                zhalo[slot] = jnp.zeros_like(zhalo[slot])
+    for load in loads[2:]:
+        load.wait()
 
     diff = [diff_ref[f] for f in range(F)]
     coup = [[coup_ref[f, g] for g in range(F)] for f in range(F)]
@@ -189,9 +266,7 @@
         for p in range(q, K):
             part = jnp.where(age == p, alpha[(p, q)], part)
         poly.append(part)
-    phase = line % phases
-    edge = jnp.where(line < phases, 0, jnp.where(line >= nline - phases, 2, 1))
-    geo = geo_ref[(phase * 3 + edge) * npen + pencil]
+    geo = geo_ref[...]
     weights = []
     for c in range(K):
         for box in range(4):
@@ -203,7 +278,6 @@
     weights = jnp.concatenate(weights, axis=0)
 
     lane = lax.broadcasted_iota(jnp.int32, (BOX, NZ), 1)
-    row = lax.broadcasted_iota(jnp.int32, (BOX, NZ), 0)
     not_first, not_last = lane > 0, lane < NZ - 1
     top, bottom = row == BOX - 1, row == 0
     half = BOX // 2
@@ -229,7 +303,7 @@
         hot = (zone == jnp.broadcast_to(zrow, (zones, NZ))).astype(jnp.float32)
         qbuf[slot] = jnp.dot(tables, hot, precision=HIGHEST, preferred_element_type=jnp.float32)
 
-    inject(zone_ref[0][0:1], nslots)
+    inject(zone_ref[0:1], nslots)
 
     for off, other in slots:
 
@@ -253,6 +327,14 @@
             off = off_of(plane)
             if off == 0 and other == 0:
                 return ref[f, plane]
+            if off != 0 and other:
+                v = corner[which, slots[(off, 1)], f]
+                distance = -plane if off < 0 else plane - depth + 1
+                if distance == 2:
+                    v = pltpu.roll(v, 4, 0)
+                if distance == 3:
+                    v = turned(v, 1 - pencil, True)
+                return jnp.where(near(1 - pencil, row) < K - distance, v, 0.0)
             v = halo[which, slots[(off, other)], f, plane - off * depth]
             return jnp.where(beyond, v, 0.0) if other else v
 
@@ -336,7 +418,7 @@
         xb, yb = box // 2, box % 2
         if xb == 0:
             slot = nslots if yb == 0 else slots[(0, 1)]
-            zrow = zone_ref[0][0:1] if yb == 0 else zhalo[slot][0:1]
+            zrow = zone_ref[0:1] if yb == 0 else zhalo[slot][0:1]
         else:
             slot = jnp.int32(0)
             for off in range(-hops, hops + 1):
@@ -401,21 +483,33 @@
         table = jnp.asarray(geometry(nline * depth, npen * rows, depth, npen, K))
         cfg = (nslab, nsec, npen, F, depth, NZ, K, zones)
         vmem = pl.BlockSpec(memory_space=pltpu.VMEM)
-        smem = pl.BlockSpec(memory_space=pltpu.SMEM)
         return pl.pallas_call(
             functools.partial(kernel, cfg),
             out_shape=(
                 jax.ShapeDtypeStruct(check.shape, jnp.float32),
                 jax.ShapeDtypeStruct((K, zones // count), jnp.float32),
             ),
-            in_specs=[vmem] * 7 + [smem] * 2 + [vmem],
+            in_specs=[pl.BlockSpec(memory_space=pltpu.HBM)] * 10,
             out_specs=(vmem, vmem),
             scratch_shapes=[
+                pltpu.VMEM(check.shape, jnp.float32),
+                pltpu.VMEM(start.shape, jnp.float32),
+                pltpu.VMEM(target.shape, jnp.float32),
+                pltpu.VMEM((rows, NZ), jnp.int32),
+                pltpu.VMEM(now.shape, jnp.float32),
+                pltpu.VMEM(nxt.shape, jnp.float32),
+                pltpu.VMEM(gain.shape, jnp.float32),
+                pltpu.SMEM(diff.shape, jnp.float32),
+                pltpu.SMEM(coup.shape, jnp.float32),
+                pltpu.VMEM(table.shape[1:], jnp.float32),
+                pltpu.VMEM((2, nslots, F, rows, NZ), jnp.float32),
                 pltpu.VMEM((2, nslots, F, depth, rows, NZ), jnp.float32),
+                pltpu.VMEM((2, nslots, F, rows, NZ), jnp.float32),
                 pltpu.VMEM((nslots, rows, NZ), jnp.int32),
                 pltpu.VMEM((nslots + 1, 2 * K + 8, NZ), jnp.float32),
                 pltpu.VMEM((count, 1, 128), jnp.float32),
                 pltpu.VMEM((count - 1, 1, 128), jnp.float32),
+                pltpu.SemaphoreType.DMA((10,)),
                 pltpu.SemaphoreType.DMA((3, nslots)),
                 pltpu.SemaphoreType.DMA((3, nslots)),
                 pltpu.SemaphoreType.DMA,

time: 33.9 us -> 29.6 us (0.87)
  Pallas kernels: 24.1 us -> 19.8 us
    pallas_call x1, Pallas kernels: 24.1 us -> 19.8 us  [per_device(): pl.pallas_call(functools.partial(kernel, cfg), out_shape=(jax.ShapeDtypeS...]
where the time goes in v2:
time: 29.6 us; the launch traced here: 29.2 us
  Pallas kernels  19.8 us (67%)
  local copies, waits for them, and re-layouts  8.67 us (29%)
  between operations  0.66 us (2%)
    pallas_call x1, Pallas kernels, per_device(): pl.pallas_call(functools.partial(kernel, cfg), out_shape=(jax.ShapeDtypeS...  19.8 us
    unnamed x22, local copies, waits for them, and re-layouts  8.67 us

profile of v2, /device:TPU:0, one launch (start us, length us, event | category | flops | bytes accessed | tf_op | source)
XLA Modules:
  0.0 29.2 jit_solution(13914468944090752929)
XLA Ops:
  0.6 0.0 copy-start
  0.6 0.9 %copy-done = f32[12,16,128]{2,1,0:T(8,128)S(1)} copy-done((f32[12,16,128]{2,1,0:T(8,128)S(1)}, f32[12,16,128]{2,1,0:T(8,128)}, u32[]{:S(2)}) %copy-start) | copy-done | bytes 98328
  1.5 0.0 copy-start.1
  1.5 0.9 %copy-done.1 = f32[5,4,8,128]{3,2,1,0:T(8,128)S(1)} copy-done((f32[5,4,8,128]{3,2,1,0:T(8,128)S(1)}, f32[5,4,8,128]{3,2,1,0:T(8,128)}, u32[]{:S(2)}) %copy-start.1) | copy-done | bytes 81944
  2.4 0.0 copy-start.2
  2.4 0.9 %copy-done.2 = f32[5,4,8,128]{3,2,1,0:T(8,128)S(1)} copy-done((f32[5,4,8,128]{3,2,1,0:T(8,128)S(1)}, f32[5,4,8,128]{3,2,1,0:T(8,128)}, u32[]{:S(2)}) %copy-start.2) | copy-done | bytes 81944
  3.3 0.0 copy-start.3
  3.3 0.7 %copy-done.3 = f32[4,8,128]{2,1,0:T(8,128)S(1)} copy-done((f32[4,8,128]{2,1,0:T(8,128)S(1)}, f32[4,8,128]{2,1,0:T(8,128)}, u32[]{:S(2)}) %copy-start.3) | copy-done | bytes 16408
  4.0 0.0 copy-start.4
  4.0 0.7 %copy-done.4 = s32[4,8,128]{2,1,0:T(8,128)S(1)} copy-done((s32[4,8,128]{2,1,0:T(8,128)S(1)}, s32[4,8,128]{2,1,0:T(8,128)}, u32[]{:S(2)}) %copy-start.4) | copy-done | bytes 16408
  4.7 0.0 copy-start.5
  4.7 0.7 %copy-done.5 = f32[5,5]{1,0:T(8,128)S(1)} copy-done((f32[5,5]{1,0:T(8,128)S(1)}, f32[5,5]{1,0:T(8,128)}, u32[]{:S(2)}) %copy-start.5) | copy-done | bytes 124
  5.4 0.0 copy-start.6
  5.4 0.7 %copy-done.6 = f32[4,64]{1,0:T(4,128)S(1)} copy-done((f32[4,64]{1,0:T(4,128)S(1)}, f32[4,64]{1,0:T(4,128)}, u32[]{:S(2)}) %copy-start.6) | copy-done | bytes 1048
  6.1 0.0 copy-start.7
  6.1 0.7 %copy-done.7 = f32[4,64]{1,0:T(4,128)S(1)} copy-done((f32[4,64]{1,0:T(4,128)S(1)}, f32[4,64]{1,0:T(4,128)}, u32[]{:S(2)}) %copy-start.7) | copy-done | bytes 1048
  6.8 0.0 copy-start.8
  6.8 0.7 %copy-done.8 = f32[64]{0:T(128)S(1)} copy-done((f32[64]{0:T(128)S(1)}, f32[64]{0:T(128)}, u32[]{:S(2)}) %copy-start.8) | copy-done | bytes 280
  7.4 0.0 copy-start.9
  7.4 0.7 %copy-done.9 = f32[5]{0:T(128)S(1)} copy-done((f32[5]{0:T(128)S(1)}, f32[5]{0:T(128)}, u32[]{:S(2)}) %copy-start.9) | copy-done | bytes 44
  8.1 19.8 %shard_map.113 = (f32[5,4,8,128]{3,2,1,0:T(8,128)S(1)}, f32[4,4]{1,0:T(4,128)S(1)}) custom-call(f32[5,4,8,128]{3,2,1,0:T(8,128)S(1)} %copy-done.1, f32[5,4,8,128]{3,2,1,0:T(8,128)S(1)} %copy-done.2, f32[4,8,128]{2,1,0:T(8,128)S(1)} %copy-done.3, s32[4,8,128]{2,1,0:T(8,128)S(1)} %copy-done.4, f32[4,64]{1,0:T(4,128)S(1)} %copy-done.6, f32[4,64]{1,0:T(4,128)S(1)} %copy-done.7, ...), custom_call_target="tpu_custom_call" | custom-call | tf_op jit(solution)/shard_map/pallas_call | solution.py:486
  27.9 0.6 %copy.14 = f32[5,4,8,128]{3,2,1,0:T(8,128)} copy(f32[5,4,8,128]{3,2,1,0:T(8,128)S(1)} %get-tuple-element.4) | data formatting | bytes 163840
  28.6 0.6 %copy.15 = f32[4,4]{1,0:T(4,128)} copy(f32[4,4]{1,0:T(4,128)S(1)} %get-tuple-element.5) | data formatting | bytes 128
Async XLA Ops:
  0.6 0.9 %copy-start = (f32[12,16,128]{2,1,0:T(8,128)S(1)}, f32[12,16,128]{2,1,0:T(8,128)}, u32[]{:S(2)}) copy-start(f32[12,16,128]{2,1,0:T(8,128)} %constant.2.clone.geo_hbm) | copy-start | bytes 294916
  1.5 0.9 %copy-start.1 = (f32[5,4,8,128]{3,2,1,0:T(8,128)S(1)}, f32[5,4,8,128]{3,2,1,0:T(8,128)}, u32[]{:S(2)}) copy-start(f32[5,4,8,128]{3,2,1,0:T(8,128)} %check_hbm.1) | copy-start | bytes 245764
  2.4 0.9 %copy-start.2 = (f32[5,4,8,128]{3,2,1,0:T(8,128)S(1)}, f32[5,4,8,128]{3,2,1,0:T(8,128)}, u32[]{:S(2)}) copy-start(f32[5,4,8,128]{3,2,1,0:T(8,128)} %start_hbm.1) | copy-start | bytes 245764
  3.3 0.7 %copy-start.3 = (f32[4,8,128]{2,1,0:T(8,128)S(1)}, f32[4,8,128]{2,1,0:T(8,128)}, u32[]{:S(2)}) copy-start(f32[4,8,128]{2,1,0:T(8,128)} %target_hbm.1) | copy-start | bytes 49156
  4.0 0.7 %copy-start.4 = (s32[4,8,128]{2,1,0:T(8,128)S(1)}, s32[4,8,128]{2,1,0:T(8,128)}, u32[]{:S(2)}) copy-start(s32[4,8,128]{2,1,0:T(8,128)} %zone_hbm.1) | copy-start | bytes 49156
  4.7 0.7 %copy-start.5 = (f32[5,5]{1,0:T(8,128)S(1)}, f32[5,5]{1,0:T(8,128)}, u32[]{:S(2)}) copy-start(f32[5,5]{1,0:T(8,128)} %coup_hbm.1) | copy-start | bytes 304
  5.4 0.7 %copy-start.6 = (f32[4,64]{1,0:T(4,128)S(1)}, f32[4,64]{1,0:T(4,128)}, u32[]{:S(2)}) copy-start(f32[4,64]{1,0:T(4,128)} %now_hbm.1) | copy-start | bytes 3076
  6.1 0.7 %copy-start.7 = (f32[4,64]{1,0:T(4,128)S(1)}, f32[4,64]{1,0:T(4,128)}, u32[]{:S(2)}) copy-start(f32[4,64]{1,0:T(4,128)} %next_hbm.1) | copy-start | bytes 3076
  6.8 0.7 %copy-start.8 = (f32[64]{0:T(128)S(1)}, f32[64]{0:T(128)}, u32[]{:S(2)}) copy-start(f32[64]{0:T(128)} %gain_hbm.1) | copy-start | bytes 772
  7.4 0.7 %copy-start.9 = (f32[5]{0:T(128)S(1)}, f32[5]{0:T(128)}, u32[]{:S(2)}) copy-start(f32[5]{0:T(128)} %diff_hbm.1) | copy-start | bytes 64

commit v3 on v2

--- a/solution.py
+++ b/solution.py
@@ -516,7 +516,7 @@
                 pltpu.SemaphoreType.DMA,
             ],
             compiler_params=pltpu.CompilerParams(
-                collective_id=0, has_side_effects=True, vmem_limit_bytes=32 * 1024 * 1024
+                collective_id=0, has_side_effects=True, vmem_limit_bytes=62 * 1024 * 1024
             ),
         )(check, start, target, zone, now, nxt, gain, diff, coup, table)
 

time: 29.6 us -> 23.6 us (0.80)
  local copies, waits for them, and re-layouts: 8.67 us -> 2.11 us
  Pallas kernels: 19.8 us -> 20.6 us
    unnamed x22 -> x4, local copies, waits for them, and re-layouts: 8.67 us -> 2.11 us
    pallas_call x1, Pallas kernels: 19.8 us -> 20.6 us  [per_device(): pl.pallas_call(functools.partial(kernel, cfg), out_shape=(jax.ShapeDtypeS...]
where the time goes in v3:
time: 23.6 us; the launch traced here: 23.4 us
  Pallas kernels  20.6 us (87%)
  local copies, waits for them, and re-layouts  2.11 us (9%)
  between operations  0.65 us (3%)
    pallas_call x1, Pallas kernels, per_device(): pl.pallas_call(functools.partial(kernel, cfg), out_shape=(jax.ShapeDtypeS...  20.6 us
    unnamed x4, local copies, waits for them, and re-layouts  2.11 us

profile of v3, /device:TPU:0, one launch (start us, length us, event | category | flops | bytes accessed | tf_op | source)
XLA Modules:
  0.0 23.4 jit_solution(10528879359271586773)
XLA Ops:
  0.6 20.6 %shard_map.113 = (f32[5,4,8,128]{3,2,1,0:T(8,128)}, f32[4,4]{1,0:T(4,128)}) custom-call(f32[5,4,8,128]{3,2,1,0:T(8,128)} %check_hbm.1, f32[5,4,8,128]{3,2,1,0:T(8,128)} %start_hbm.1, f32[4,8,128]{2,1,0:T(8,128)} %target_hbm.1, s32[4,8,128]{2,1,0:T(8,128)} %zone_hbm.1, f32[4,64]{1,0:T(4,128)} %now_hbm.1, f32[4,64]{1,0:T(4,128)} %next_hbm.1, f32[64]{0:T(128)} %gain_hbm.1, ...), custom_call_target="tpu_custom_call" | custom-call | tf_op jit(solution)/shard_map/pallas_call | solution.py:486
  21.2 0.0 copy-start
  21.3 1.5 %copy.14 = f32[5,4,8,128]{3,2,1,0:T(8,128)} copy(f32[5,4,8,128]{3,2,1,0:T(8,128)} %get-tuple-element.4) | data formatting | bytes 163840
  22.8 0.0 copy-done
  22.8 0.6 %copy.15 = f32[4,4]{1,0:T(4,128)} copy(f32[4,4]{1,0:T(4,128)S(1)} %copy-done) | data formatting | bytes 128
Async XLA Ops:
  21.2 1.5 %copy-start = (f32[4,4]{1,0:T(4,128)S(1)}, f32[4,4]{1,0:T(4,128)}, u32[]{:S(2)}) copy-start(f32[4,4]{1,0:T(4,128)} %get-tuple-element.5) | copy-start | bytes 196

commit v4 on v3

--- a/solution.py
+++ b/solution.py
@@ -86,6 +86,7 @@
     load_sem,
     halo_send,
     halo_recv,
+    ready,
     sum_send,
     sum_recv,
 ):
@@ -133,17 +134,45 @@
 
     barrier = pltpu.get_barrier_semaphore()
 
-    def greet(r, carry):
-        peer = lax.rem(me + r, count)
-        pl.semaphore_signal(
-            barrier, inc=1, device_id=where_is(peer // npen, peer % npen), device_id_type=MESH
-        )
-        return carry
-
-    lax.fori_loop(1, count, greet, 0)
-
     def exists(off):
         return jnp.logical_and(line + off >= 0, line + off < nline)
+
+    expected = 0
+    for off, other in slots:
+        expected = expected + exists(off).astype(jnp.int32)
+
+        @pl.when(exists(off))
+        def _(off=off, other=other):
+            pl.semaphore_signal(
+                barrier,
+                inc=1,
+                device_id=where_is(line + off, pencil if other == 0 else 1 - pencil),
+                device_id_type=MESH,
+            )
+
+    strides = []
+    reach = hops
+    while reach < nline - 1:
+        strides.append(reach)
+        reach *= 2
+
+    def tell(stage):
+        for off in (-strides[stage], strides[stage]):
+
+            @pl.when(exists(off))
+            def _(off=off):
+                pl.semaphore_signal(
+                    ready.at[stage],
+                    inc=1,
+                    device_id=where_is(line + off, pencil),
+                    device_id_type=MESH,
+                )
+
+    def hear(stage):
+        far = strides[stage]
+        pl.semaphore_wait(
+            ready.at[stage], exists(-far).astype(jnp.int32) + exists(far).astype(jnp.int32)
+        )
 
     for off, other in slots:
         if off != 0:
@@ -194,7 +223,9 @@
     pack(0, check_ref)
     loads[1].wait()
     pack(1, start_ref)
-    pl.semaphore_wait(barrier, count - 1)
+    pl.semaphore_wait(barrier, expected)
+    if strides:
+        tell(0)
 
     def copy_to(what, off, other, arriving):
         here = slots[(off, other)]
@@ -223,6 +254,11 @@
 
     for load in loads[2:]:
         load.wait()
+
+    for stage in range(len(strides)):
+        hear(stage)
+        if stage + 1 < len(strides):
+            tell(stage + 1)
 
     diff = [diff_ref[f] for f in range(F)]
     coup = [[coup_ref[f, g] for g in range(F)] for f in range(F)]
@@ -512,6 +548,7 @@
                 pltpu.SemaphoreType.DMA((10,)),
                 pltpu.SemaphoreType.DMA((3, nslots)),
                 pltpu.SemaphoreType.DMA((3, nslots)),
+                pltpu.SemaphoreType.REGULAR((max(1, nline.bit_length()),)),
                 pltpu.SemaphoreType.DMA,
                 pltpu.SemaphoreType.DMA,
             ],

time: 23.6 us -> 22.9 us (0.970)
  Pallas kernels: 20.6 us -> 19.9 us
    pallas_call x1, Pallas kernels: 20.6 us -> 19.9 us  [per_device(): pl.pallas_call(functools.partial(kernel, cfg), out_shape=(jax.ShapeDtypeS...]
where the time goes in v4:
time: 22.9 us; the launch traced here: 22.7 us
  Pallas kernels  19.9 us (87%)
  local copies, waits for them, and re-layouts  2.11 us (9%)
  between operations  0.65 us (3%)
    pallas_call x1, Pallas kernels, per_device(): pl.pallas_call(functools.partial(kernel, cfg), out_shape=(jax.ShapeDtypeS...  19.9 us
    unnamed x4, local copies, waits for them, and re-layouts  2.11 us

profile of v4, /device:TPU:0, one launch (start us, length us, event | category | flops | bytes accessed | tf_op | source)
XLA Modules:
  0.0 22.7 jit_solution(3206051673293590821)
XLA Ops:
  0.6 19.9 %shard_map.113 = (f32[5,4,8,128]{3,2,1,0:T(8,128)}, f32[4,4]{1,0:T(4,128)}) custom-call(f32[5,4,8,128]{3,2,1,0:T(8,128)} %check_hbm.1, f32[5,4,8,128]{3,2,1,0:T(8,128)} %start_hbm.1, f32[4,8,128]{2,1,0:T(8,128)} %target_hbm.1, s32[4,8,128]{2,1,0:T(8,128)} %zone_hbm.1, f32[4,64]{1,0:T(4,128)} %now_hbm.1, f32[4,64]{1,0:T(4,128)} %next_hbm.1, f32[64]{0:T(128)} %gain_hbm.1, ...), custom_call_target="tpu_custom_call" | custom-call | tf_op jit(solution)/shard_map/pallas_call | solution.py:522
  20.5 0.0 copy-start
  20.6 1.5 %copy.14 = f32[5,4,8,128]{3,2,1,0:T(8,128)} copy(f32[5,4,8,128]{3,2,1,0:T(8,128)} %get-tuple-element.4) | data formatting | bytes 163840
  22.1 0.0 copy-done
  22.1 0.6 %copy.15 = f32[4,4]{1,0:T(4,128)} copy(f32[4,4]{1,0:T(4,128)S(1)} %copy-done) | data formatting | bytes 128
Async XLA Ops:
  20.5 1.5 %copy-start = (f32[4,4]{1,0:T(4,128)S(1)}, f32[4,4]{1,0:T(4,128)}, u32[]{:S(2)}) copy-start(f32[4,4]{1,0:T(4,128)} %get-tuple-element.5) | copy-start | bytes 196

commit v5 on v4

--- a/solution.py
+++ b/solution.py
@@ -187,6 +187,12 @@
                         halo[which, slot] = jnp.zeros_like(halo[which, slot])
                 zhalo[slot] = jnp.zeros_like(zhalo[slot])
 
+    for off in (-hops, hops):
+        far = 0 if off < 0 else depth - 1
+        if hops * depth == K:
+            slot = slots[(off, 0)]
+            halo[0, slot, 1:, far] = jnp.zeros((F - 1, BOX, NZ), jnp.float32)
+
     row = lax.broadcasted_iota(jnp.int32, (BOX, NZ), 0)
 
     def near(pen, at):
@@ -232,6 +238,12 @@
         slot = here if arriving else slots[(-off, other)]
         if what == 0:
             src, dst = zone_hbm.at[0], zhalo.at[slot]
+        elif what == 3:
+            far = plane_at(-off if arriving else off, K)
+            src, dst = check_hbm.at[0, far], halo.at[0, slot, 0, far]
+        elif what == 1 and not other and abs(off) == hops:
+            planes = pl.ds(0 if plane_at(-off if arriving else off, K) else 1, depth - 1)
+            src, dst = check_hbm.at[:, planes], halo.at[0, slot, :, planes]
         elif off != 0 and other:
             src, dst = packed.at[what - 1, here], corner.at[what - 1, slot]
         else:
@@ -245,8 +257,11 @@
             device_id_type=MESH,
         )
 
-    for what in range(3):
-        for off, other in slots:
+    def places(what):
+        return [key for key in slots if what != 3 or (key[1] == 0 and abs(key[0]) == hops)]
+
+    for what in (0, 1, 3, 2):
+        for off, other in places(what):
 
             @pl.when(exists(off))
             def _(off=off, other=other, what=what):
@@ -255,10 +270,14 @@
     for load in loads[2:]:
         load.wait()
 
-    for stage in range(len(strides)):
-        hear(stage)
-        if stage + 1 < len(strides):
-            tell(stage + 1)
+    def pass_on(stages):
+        for stage in stages:
+            hear(stage)
+            if stage + 1 < len(strides):
+                tell(stage + 1)
+
+    last = len(strides) - 1
+    pass_on(range(min(1, last)))
 
     diff = [diff_ref[f] for f in range(F)]
     coup = [[coup_ref[f, g] for g in range(F)] for f in range(F)]
@@ -352,6 +371,7 @@
     for off, other in slots:
         slot = slots[(off, other)]
         inject(zhalo[slot][0:1], slot)
+    pass_on(range(min(1, last), last))
 
     inside = {off: jnp.where(exists(off), 1.0, 0.0) for off in range(-hops, hops + 1)}
 
@@ -416,7 +436,7 @@
         return T
 
     def wait_halo(what):
-        for off, other in slots:
+        for off, other in places(what):
 
             @pl.when(exists(off))
             def _(off=off, other=other):
@@ -425,6 +445,7 @@
                 copy.wait_recv()
 
     wait_halo(1)
+    wait_halo(3)
     misfits = []
 
     def seen(T):
@@ -491,6 +512,7 @@
         ).start()
         return carry
 
+    pass_on(range(max(last, 0), last + 1))
     lax.fori_loop(1, count, give, 0)
 
     wait_halo(2)
@@ -546,8 +568,8 @@
                 pltpu.VMEM((count, 1, 128), jnp.float32),
                 pltpu.VMEM((count - 1, 1, 128), jnp.float32),
                 pltpu.SemaphoreType.DMA((10,)),
-                pltpu.SemaphoreType.DMA((3, nslots)),
-                pltpu.SemaphoreType.DMA((3, nslots)),
+                pltpu.SemaphoreType.DMA((4, nslots)),
+                pltpu.SemaphoreType.DMA((4, nslots)),
                 pltpu.SemaphoreType.REGULAR((max(1, nline.bit_length()),)),
                 pltpu.SemaphoreType.DMA,
                 pltpu.SemaphoreType.DMA,

time: 22.9 us -> 22.7 us (level)
  no operation moved by 1% of the time
where the time goes in v5:
time: 22.7 us; the launch traced here: 22.5 us
  Pallas kernels  19.8 us (87%)
  local copies, waits for them, and re-layouts  2.11 us (9%)
  between operations  0.65 us (3%)
    pallas_call x1, Pallas kernels, per_device(): pl.pallas_call(functools.partial(kernel, cfg), out_shape=(jax.ShapeDtypeS...  19.8 us
    unnamed x4, local copies, waits for them, and re-layouts  2.11 us

profile of v5, /device:TPU:0, one launch (start us, length us, event | category | flops | bytes accessed | tf_op | source)
XLA Modules:
  0.0 22.5 jit_solution(10256656847138165444)
XLA Ops:
  0.6 19.8 %shard_map.113 = (f32[5,4,8,128]{3,2,1,0:T(8,128)}, f32[4,4]{1,0:T(4,128)}) custom-call(f32[5,4,8,128]{3,2,1,0:T(8,128)} %check_hbm.1, f32[5,4,8,128]{3,2,1,0:T(8,128)} %start_hbm.1, f32[4,8,128]{2,1,0:T(8,128)} %target_hbm.1, s32[4,8,128]{2,1,0:T(8,128)} %zone_hbm.1, f32[4,64]{1,0:T(4,128)} %now_hbm.1, f32[4,64]{1,0:T(4,128)} %next_hbm.1, f32[64]{0:T(128)} %gain_hbm.1, ...), custom_call_target="tpu_custom_call" | custom-call | tf_op jit(solution)/shard_map/pallas_call | solution.py:544
  20.4 0.0 copy-start
  20.4 1.5 %copy.14 = f32[5,4,8,128]{3,2,1,0:T(8,128)} copy(f32[5,4,8,128]{3,2,1,0:T(8,128)} %get-tuple-element.4) | data formatting | bytes 163840
  21.9 0.0 copy-done
  21.9 0.6 %copy.15 = f32[4,4]{1,0:T(4,128)} copy(f32[4,4]{1,0:T(4,128)S(1)} %copy-done) | data formatting | bytes 128
Async XLA Ops:
  20.4 1.5 %copy-start = (f32[4,4]{1,0:T(4,128)S(1)}, f32[4,4]{1,0:T(4,128)}, u32[]{:S(2)}) copy-start(f32[4,4]{1,0:T(4,128)} %get-tuple-element.5) | copy-start | bytes 196
